TPU v7x, 32 devices: a whole 2x2x4 slice. The times are simulated.
32 devices in a mesh: dp: 4 (over y, x), vocab: 8 (over z, core).
Axes of the slice: x: 2, y: 2, z: 4, core: 2. Of those that a mesh axis runs over, the one named last changes fastest.
Arguments:
- hidden: bfloat16 [128, 3584], P(('dp', 'vocab')), may hold values from -6 to 6
- head_weight: bfloat16 [3584, 256000], P(None, ('dp', 'vocab')), may hold values from -0.75 to 0.75
- teacher_ids: int32 [128, 128], P(('dp', 'vocab')), may hold values from 0 to 255999
- teacher_probs: float32 [128, 128], P(('dp', 'vocab')), may hold values from 0.0001 to 0.015
- target_ids: int32 [128], P(('dp', 'vocab')), may hold values from 0 to 255999
Outputs:
- token_loss: float32 [128], P(('dp', 'vocab'))
- hidden_grad: bfloat16 [128, 3584], P(('dp', 'vocab'))
All inputs are finite; a program needn't handle non-finite values.
Results may differ from a plain program's by a relative error of at most 0.004.
Values may be sent and summed in bfloat16 or wider, within the bound.
A program may use at most 128 MiB of HBM per device.

v0:
```python
import jax
import jax.numpy as jnp
from jax import lax
from jax.sharding import PartitionSpec as P

SOFT_CAP = 30.0
CE_WEIGHT = 0.5
LOSS_SCALE = 8.0
BLOCK_ROWS = 32


def sparse_rows(teacher_ids, teacher_probs, columns):
    token_count, kept = teacher_ids.shape
    block_rows = BLOCK_ROWS
    id_blocks = teacher_ids.reshape(token_count // block_rows, block_rows, kept)
    prob_blocks = teacher_probs.reshape(token_count // block_rows, block_rows, kept)

    def one_block(pair):
        id_rows, prob_rows = pair
        match = id_rows[:, :, None] == columns[None, None, :]
        return jnp.sum(jnp.where(match, prob_rows[:, :, None], 0.0), axis=1)

    summed = lax.map(one_block, (id_blocks, prob_blocks))
    return summed.reshape(token_count, columns.shape[0])


def per_device(hidden, head_weight, teacher_ids, teacher_probs, target_ids):
    slice_width = head_weight.shape[1]
    tokens_local = hidden.shape[0]
    position = lax.axis_index(("dp", "vocab"))
    first_column = position * slice_width
    columns = first_column + jnp.arange(slice_width, dtype=jnp.int32)
    raw_logits = jnp.dot(
        lax.all_gather(hidden, ("dp", "vocab"), axis=0, tiled=True),
        head_weight,
        preferred_element_type=jnp.float32,
    )
    capped = SOFT_CAP * jnp.tanh(raw_logits / SOFT_CAP)
    all_ids, all_targets = (
        lax.all_gather(teacher_ids, ("dp", "vocab"), axis=0, tiled=True),
        lax.all_gather(target_ids, ("dp", "vocab"), axis=0, tiled=True),
    )
    all_probs = lax.all_gather(teacher_probs, ("dp", "vocab"), axis=0, tiled=True)
    sparse = sparse_rows(all_ids, all_probs, columns)
    target_hit = columns[None, :] == all_targets[:, None]
    part_dot = jnp.sum(capped * sparse, axis=1)
    part_target = jnp.sum(jnp.where(target_hit, capped, 0.0), axis=1)
    part_exp = jnp.sum(jnp.exp(capped), axis=1)
    exp_sum, teacher_dot, target_logit = lax.psum(
        (part_exp, part_dot, part_target), ("dp", "vocab")
    )
    log_total = jnp.log(exp_sum)
    teacher_sum = jnp.sum(all_probs, axis=1)
    every_loss = (
        jnp.sum(all_probs * jnp.log(all_probs), axis=1)
        - teacher_dot
        + teacher_sum * log_total
        + CE_WEIGHT * (log_total - target_logit)
    )
    token_loss = lax.dynamic_slice_in_dim(every_loss, position * tokens_local, tokens_local)
    softmax_rows = jnp.exp(capped - log_total[:, None])
    onehot = jnp.where(target_hit, 1.0, 0.0)
    raw_grads = LOSS_SCALE * (
        (teacher_sum + CE_WEIGHT)[:, None] * softmax_rows - sparse - CE_WEIGHT * onehot
    )
    grads = (raw_grads * (1.0 - (capped / SOFT_CAP) ** 2)).astype(jnp.bfloat16)
    summed = lax.psum_scatter(
        jnp.einsum("tv,dv->td", grads, head_weight, preferred_element_type=jnp.float32),
        ("dp", "vocab"),
        scatter_dimension=0,
        tiled=True,
    )
    return (token_loss, summed.astype(jnp.bfloat16))


def solution(mesh):
    in_specs = (
        P(("dp", "vocab"), None),
        P(None, ("dp", "vocab")),
        P(("dp", "vocab"), None),
        P(("dp", "vocab"), None),
        P(("dp", "vocab")),
    )
    out_specs = (P(("dp", "vocab")), P(("dp", "vocab"), None))
    return jax.shard_map(
        per_device, mesh=mesh, in_specs=in_specs, out_specs=out_specs, check_vma=False
    )
```

profile of v0, /device:TPU:0, one launch (start us, length us, event | category | flops | bytes accessed | tf_op | source)
XLA Modules:
  0.0 491.0 jit_solution(7940874425076551939)
XLA Ops:
  0.6 0.9 dynamic-update-slice
  1.5 42.0 %all-reduce = s32[128]{0:T(128)S(1)} all-reduce(s32[128]{0:T(128)S(1)} %dynamic-update-slice), channel_id=1, replica_groups=mesh['dp'=4,'vocab'=8] {'dp','vocab'}, use_global_device_ids=true, to_apply=%add | all-reduce | flops 128 | bytes 1024
  43.5 40.7 %all-gather.2 = s32[32,4,128]{2,1,0:T(4,128)S(1)} all-gather(s32[1,4,128]{2,1,0:T(4,128)} %bitcast.28), channel_id=1, replica_groups=mesh['dp'=4,'vocab'=8] {'dp','vocab'}, dimensions={0}, use_global_device_ids=true | all-gather | bytes 67584 | tf_op jit(solution)/shard_map/all_gather | solution.py:40
  84.2 37.1 %all-gather = f32[32,4,128]{2,1,0:T(4,128)S(1)} all-gather(f32[1,4,128]{2,1,0:T(4,128)} %bitcast.29), channel_id=1, replica_groups=mesh['dp'=4,'vocab'=8] {'dp','vocab'}, dimensions={0}, use_global_device_ids=true | all-gather | bytes 67584 | tf_op jit(solution)/shard_map/all_gather | solution.py:43
  121.3 171.5 %while.11 = (s32[]{:T(128)}, f32[4,32,8000]{2,1,0:T(8,128)}, s32[4,32,128]{2,1,0:T(8,128)S(1)}, f32[4,32,128]{2,1,0:T(8,128)S(1)}, s32[]{:T(128)}, /*index=5*/s32[]{:T(128)}) while((s32[]{:T(128)}, f32[4,32,8000]{2,1,0:T(8,128)}, s32[4,32,128]{2,1,0:T(8,128)S(1)}, f32[4,32,128]{2,1,0:T(8,128)S(1)}, s32[]{:T(128)}, ...), condition=%wide.region_3.4_spmd.clone, body=%wide.region_1.3_spmd.clone.sunk | while | flops 98056000 | bytes 3242589 | solution.py:23
  121.3 41.8 %select_reduce_fusion.2 = f32[32,8000]{1,0:T(8,128)S(1)} fusion(f32[32,128]{1,0:T(8,128)S(1)} %dynamic-slice_bitcast_fusion.4, s32[32,128]{1,0:T(8,128)S(1)} %dynamic-slice_bitcast_fusion.5, s32[8000]{0:T(1024)S(1)} %iota_add_fusion.3), kind=kLoop, calls=%fused_computation.1.clone.1 | loop fusion | flops 98048000 | bytes 1088768 | tf_op jit(solution)/shard_map/while/body/eval_jaxpr/reduce_sum | solution.py:21
  163.1 1.1 bitcast_dynamic-update-slice_fusion.2
  164.1 41.8 %select_reduce_fusion.2 = f32[32,8000]{1,0:T(8,128)S(1)} fusion(f32[32,128]{1,0:T(8,128)S(1)} %dynamic-slice_bitcast_fusion.4, s32[32,128]{1,0:T(8,128)S(1)} %dynamic-slice_bitcast_fusion.5, s32[8000]{0:T(1024)S(1)} %iota_add_fusion.3), kind=kLoop, calls=%fused_computation.1.clone.1 | loop fusion | flops 98048000 | bytes 1088768 | tf_op jit(solution)/shard_map/while/body/eval_jaxpr/reduce_sum | solution.py:21
  205.9 1.1 bitcast_dynamic-update-slice_fusion.2
  207.0 41.8 %select_reduce_fusion.2 = f32[32,8000]{1,0:T(8,128)S(1)} fusion(f32[32,128]{1,0:T(8,128)S(1)} %dynamic-slice_bitcast_fusion.4, s32[32,128]{1,0:T(8,128)S(1)} %dynamic-slice_bitcast_fusion.5, s32[8000]{0:T(1024)S(1)} %iota_add_fusion.3), kind=kLoop, calls=%fused_computation.1.clone.1 | loop fusion | flops 98048000 | bytes 1088768 | tf_op jit(solution)/shard_map/while/body/eval_jaxpr/reduce_sum | solution.py:21
  248.8 1.0 bitcast_dynamic-update-slice_fusion.2
  249.9 41.8 %select_reduce_fusion.2 = f32[32,8000]{1,0:T(8,128)S(1)} fusion(f32[32,128]{1,0:T(8,128)S(1)} %dynamic-slice_bitcast_fusion.4, s32[32,128]{1,0:T(8,128)S(1)} %dynamic-slice_bitcast_fusion.5, s32[8000]{0:T(1024)S(1)} %iota_add_fusion.3), kind=kLoop, calls=%fused_computation.1.clone.1 | loop fusion | flops 98048000 | bytes 1088768 | tf_op jit(solution)/shard_map/while/body/eval_jaxpr/reduce_sum | solution.py:21
  291.7 1.0 bitcast_dynamic-update-slice_fusion.2
  292.7 5.6 %copy.12 = f32[128,8000]{0,1:T(8,128)} copy(f32[128,8000]{1,0:T(8,128)} %bitcast.22) | data formatting | bytes 8192000 | tf_op jit(solution)/shard_map/reshape | solution.py:24
  298.4 41.8 %all-gather.1 = bf16[32,4,3584]{2,1,0:T(4,128)(2,1)S(1)} all-gather(bf16[1,4,3584]{2,1,0:T(4,128)(2,1)S(1)} %bitcast.27), channel_id=1, replica_groups=mesh['dp'=4,'vocab'=8] {'dp','vocab'}, dimensions={0}, use_global_device_ids=true | all-gather | bytes 946176 | tf_op jit(solution)/shard_map/all_gather | solution.py:34
  340.2 0.2 reshape.35
  340.4 25.1 %exponential_reduce_fusion = (f32[128]{0:T(128)S(1)}, f32[128]{0:T(128)S(1)}, f32[128]{0:T(128)S(1)}, f32[128,8000]{0,1:T(8,128)}) fusion(s32[128]{0:T(128)S(1)} %all-reduce, s32[8000]{0:T(1024)S(1)} %iota_add_fusion.1, f32[128,8000]{0,1:T(8,128)} %copy.12, bf16[128,3584]{1,0:T(8,128)(2,1)S(1)} %reshape.35, bf16[3584,8000]{0,1:T(8,128)(2,1)} %param.8), kind=kOutput, calls=%fused_computation.16 | convolution fusion | flops 7348224000 | bytes 66487552 | tf_op jit(solution)/shard_map/dot_general | solution.py:33
  365.6 37.9 %psum.22 = f32[128]{0:T(128)S(1)} all-reduce(f32[128]{0:T(128)S(1)} %get-tuple-element.43), channel_id=1, replica_groups=mesh['dp'=4,'vocab'=8] {'dp','vocab'}, use_global_device_ids=true, to_apply=%region_8.9 | all-reduce | flops 128 | bytes 1024 | tf_op jit(solution)/shard_map/psum | solution.py:49
  403.4 0.1 reduce
  403.7 23.4 %fusion.9 = f32[128,3584]{1,0:T(8,128)S(1)} fusion(bf16[3584,8000]{0,1:T(8,128)(2,1)} %param.8, f32[128,8000]{0,1:T(8,128)} %get-tuple-element.59, f32[128,8000]{0,1:T(8,128)} %copy.12, f32[128]{0:T(128)S(1)} %log.7, f32[128]{0:T(128)S(1)} %broadcast_add_fusion, s32[128]{0:T(128)S(1)} %all-reduce, s32[8000]{0:T(1024)S(1)} %iota_add_fusion.1), kind=kOutput, calls=%fused_computation.18 | convolution fusion | flops 7353344000 | bytes 67404544 | tf_op jit(solution)/shard_map/tv,dv->td/dot_general | solution.py:68
  427.1 62.6 %all-reduce.4 = (f32[128]{0:T(128)S(1)}, f32[128]{0:T(128)S(1)}, bf16[128,3584]{1,0:T(8,128)(2,1)S(1)}) all-reduce(f32[128]{0:T(128)S(1)} %get-tuple-element.44, f32[128]{0:T(128)S(1)} %get-tuple-element.45, f32[128,3584]{1,0:T(8,128)S(1)} %fusion.9), channel_id=1, replica_groups=mesh['dp'=4,'vocab'=8] {'dp','vocab'}, use_global_device_ids=true, to_apply=%region_10.11 | all-reduce | flops 459008 | bytes 2754560 | tf_op jit(solution)/shard_map/psum | solution.py:49
  489.7 0.1 fusion.20
  489.8 0.6 dynamic_slice.11
  490.4 0.6 dynamic-slice_convert_fusion
  (21 shorter events, 0.2 us)
Async XLA Ops:
  292.7 5.6 %copy-start = (bf16[4,3584]{1,0:T(4,128)(2,1)S(1)}, bf16[4,3584]{1,0:T(4,128)(2,1)}, u32[]{:S(2)}) copy-start(bf16[4,3584]{1,0:T(4,128)(2,1)} %param.7) | copy-start | bytes 86020
where the time goes:
time: 492 us; the launch traced here: 491 us
  blocking collectives  262 us (53%)
  other arithmetic  167 us (34%)
  matrix products  48.5 us (10%)
  local copies, waits for them, and re-layouts  12.3 us (2%)
    reduce_sum x4, other arithmetic, one_block(): return jnp.sum(jnp.where(match, prob_rows[:, :, None], 0.0), axis=1)  167 us
    psum x2, blocking collectives, per_device(): lax.psum((part_exp, part_dot, part_target), ('dp', 'vocab'))  100 us
    unnamed x1, blocking collectives  42 us
    all_gather x1, blocking collectives, per_device(): lax.all_gather(hidden, ('dp', 'vocab'), axis=0, tiled=True)  41.8 us
    all_gather x1, blocking collectives, per_device(): lax.all_gather(teacher_ids, ('dp', 'vocab'), axis=0, tiled=True)  40.7 us
    all_gather x1, blocking collectives, per_device(): lax.all_gather(teacher_probs, ('dp', 'vocab'), axis=0, tiled=True)  37.1 us
    dot_general x1, matrix products, per_device(): jnp.dot(lax.all_gather(hidden, ('dp', 'vocab'), axis=0, tiled=True), head...  25.1 us
    dot_general x1, matrix products, per_device(): jnp.einsum('tv,dv->td', grads, head_weight, preferred_element_type=jnp.fl...  23.4 us

commit v1 on v0

--- a/solution.py
+++ b/solution.py
@@ -2,11 +2,16 @@
 import jax.numpy as jnp
 from jax import lax
 from jax.sharding import PartitionSpec as P
+from jax.lax import psum
 
 SOFT_CAP = 30.0
 CE_WEIGHT = 0.5
 LOSS_SCALE = 8.0
 BLOCK_ROWS = 32
+
+
+def cover_cards(a0, shard_axis, net_axis):
+    return psum(psum(a0, axis_name=shard_axis), axis_name=net_axis)
 
 
 def sparse_rows(teacher_ids, teacher_probs, columns):
@@ -46,8 +51,8 @@
     part_dot = jnp.sum(capped * sparse, axis=1)
     part_target = jnp.sum(jnp.where(target_hit, capped, 0.0), axis=1)
     part_exp = jnp.sum(jnp.exp(capped), axis=1)
-    exp_sum, teacher_dot, target_logit = lax.psum(
-        (part_exp, part_dot, part_target), ("dp", "vocab")
+    exp_sum, teacher_dot, target_logit = cover_cards(
+        (part_exp, part_dot, part_target), "vocab", "dp"
     )
     log_total = jnp.log(exp_sum)
     teacher_sum = jnp.sum(all_probs, axis=1)

time: 492 us -> 472 us (0.959)
  blocking collectives: 262 us -> 242 us
    psum x2, blocking collectives: 100 us -> 23.4 us  [cover_cards(): return psum(psum(a0, axis_name=shard_axis), axis_name=net_axis)]
    unnamed x1 -> x2, blocking collectives: 42 us -> 93.9 us
    all_gather x1, blocking collectives: 37.1 us -> 43.7 us  [per_device(): lax.all_gather(teacher_probs, ('dp', 'vocab'), axis=0, tiled=True)]
where the time goes in v1:
time: 472 us; the launch traced here: 471 us
  blocking collectives  242 us (51%)
  other arithmetic  167 us (35%)
  matrix products  48.5 us (10%)
  local copies, waits for them, and re-layouts  12.3 us (3%)
    reduce_sum x4, other arithmetic, one_block(): return jnp.sum(jnp.where(match, prob_rows[:, :, None], 0.0), axis=1)  167 us
    unnamed x2, blocking collectives  93.9 us
    all_gather x1, blocking collectives, per_device(): lax.all_gather(teacher_probs, ('dp', 'vocab'), axis=0, tiled=True)  43.7 us
    all_gather x1, blocking collectives, per_device(): lax.all_gather(teacher_ids, ('dp', 'vocab'), axis=0, tiled=True)  40.7 us
    all_gather x1, blocking collectives, per_device(): lax.all_gather(hidden, ('dp', 'vocab'), axis=0, tiled=True)  40.6 us
    dot_general x1, matrix products, per_device(): jnp.dot(lax.all_gather(hidden, ('dp', 'vocab'), axis=0, tiled=True), head...  25.2 us
    psum x2, blocking collectives, cover_cards(): return psum(psum(a0, axis_name=shard_axis), axis_name=net_axis)  23.4 us
    dot_general x1, matrix products, per_device(): jnp.einsum('tv,dv->td', grads, head_weight, preferred_element_type=jnp.fl...  23.4 us

profile of v1, /device:TPU:0, one launch (start us, length us, event | category | flops | bytes accessed | tf_op | source)
XLA Modules:
  0.0 471.4 jit_solution(6494786810547052619)
XLA Ops:
  0.6 43.7 %all-gather = f32[32,4,128]{2,1,0:T(4,128)S(1)} all-gather(f32[1,4,128]{2,1,0:T(4,128)} %bitcast.27), channel_id=1, replica_groups=mesh['dp'=4,'vocab'=8] {'dp','vocab'}, dimensions={0}, use_global_device_ids=true | all-gather | bytes 67584 | tf_op jit(solution)/shard_map/all_gather | solution.py:48
  44.6 0.9 dynamic-update-slice
  45.4 36.9 %all-reduce = s32[128]{0:T(128)S(1)} all-reduce(s32[128]{0:T(128)S(1)} %dynamic-update-slice), channel_id=1, replica_groups=mesh['dp'=4,'vocab'=8] {'dp','vocab'}, use_global_device_ids=true, to_apply=%add | all-reduce | flops 128 | bytes 1024
  82.3 40.7 %all-gather.2 = s32[32,4,128]{2,1,0:T(4,128)S(1)} all-gather(s32[1,4,128]{2,1,0:T(4,128)} %bitcast.28), channel_id=1, replica_groups=mesh['dp'=4,'vocab'=8] {'dp','vocab'}, dimensions={0}, use_global_device_ids=true | all-gather | bytes 67584 | tf_op jit(solution)/shard_map/all_gather | solution.py:45
  123.0 171.5 %while.11 = (s32[]{:T(128)}, f32[4,32,8000]{2,1,0:T(8,128)}, s32[4,32,128]{2,1,0:T(8,128)S(1)}, f32[4,32,128]{2,1,0:T(8,128)S(1)}, s32[]{:T(128)}, /*index=5*/s32[]{:T(128)}) while((s32[]{:T(128)}, f32[4,32,8000]{2,1,0:T(8,128)}, s32[4,32,128]{2,1,0:T(8,128)S(1)}, f32[4,32,128]{2,1,0:T(8,128)S(1)}, s32[]{:T(128)}, ...), condition=%wide.region_3.4_spmd.clone, body=%wide.region_1.3_spmd.clone.sunk | while | flops 98056000 | bytes 3242589 | solution.py:28
  123.1 41.8 %select_reduce_fusion.2 = f32[32,8000]{1,0:T(8,128)S(1)} fusion(f32[32,128]{1,0:T(8,128)S(1)} %dynamic-slice_bitcast_fusion.4, s32[32,128]{1,0:T(8,128)S(1)} %dynamic-slice_bitcast_fusion.5, s32[8000]{0:T(1024)S(1)} %iota_add_fusion.3), kind=kLoop, calls=%fused_computation.1.clone.1 | loop fusion | flops 98048000 | bytes 1088768 | tf_op jit(solution)/shard_map/while/body/eval_jaxpr/reduce_sum | solution.py:26
  164.9 1.1 bitcast_dynamic-update-slice_fusion.2
  165.9 41.8 %select_reduce_fusion.2 = f32[32,8000]{1,0:T(8,128)S(1)} fusion(f32[32,128]{1,0:T(8,128)S(1)} %dynamic-slice_bitcast_fusion.4, s32[32,128]{1,0:T(8,128)S(1)} %dynamic-slice_bitcast_fusion.5, s32[8000]{0:T(1024)S(1)} %iota_add_fusion.3), kind=kLoop, calls=%fused_computation.1.clone.1 | loop fusion | flops 98048000 | bytes 1088768 | tf_op jit(solution)/shard_map/while/body/eval_jaxpr/reduce_sum | solution.py:26
  207.7 1.1 bitcast_dynamic-update-slice_fusion.2
  208.8 41.8 %select_reduce_fusion.2 = f32[32,8000]{1,0:T(8,128)S(1)} fusion(f32[32,128]{1,0:T(8,128)S(1)} %dynamic-slice_bitcast_fusion.4, s32[32,128]{1,0:T(8,128)S(1)} %dynamic-slice_bitcast_fusion.5, s32[8000]{0:T(1024)S(1)} %iota_add_fusion.3), kind=kLoop, calls=%fused_computation.1.clone.1 | loop fusion | flops 98048000 | bytes 1088768 | tf_op jit(solution)/shard_map/while/body/eval_jaxpr/reduce_sum | solution.py:26
  250.6 1.0 bitcast_dynamic-update-slice_fusion.2
  251.7 41.8 %select_reduce_fusion.2 = f32[32,8000]{1,0:T(8,128)S(1)} fusion(f32[32,128]{1,0:T(8,128)S(1)} %dynamic-slice_bitcast_fusion.4, s32[32,128]{1,0:T(8,128)S(1)} %dynamic-slice_bitcast_fusion.5, s32[8000]{0:T(1024)S(1)} %iota_add_fusion.3), kind=kLoop, calls=%fused_computation.1.clone.1 | loop fusion | flops 98048000 | bytes 1088768 | tf_op jit(solution)/shard_map/while/body/eval_jaxpr/reduce_sum | solution.py:26
  293.5 1.0 bitcast_dynamic-update-slice_fusion.2
  294.5 5.6 %copy.12 = f32[128,8000]{0,1:T(8,128)} copy(f32[128,8000]{1,0:T(8,128)} %bitcast.22) | data formatting | bytes 8192000 | tf_op jit(solution)/shard_map/reshape | solution.py:29
  300.2 40.6 %all-gather.1 = bf16[32,4,3584]{2,1,0:T(4,128)(2,1)S(1)} all-gather(bf16[1,4,3584]{2,1,0:T(4,128)(2,1)S(1)} %bitcast.26), channel_id=1, replica_groups=mesh['dp'=4,'vocab'=8] {'dp','vocab'}, dimensions={0}, use_global_device_ids=true | all-gather | bytes 946176 | tf_op jit(solution)/shard_map/all_gather | solution.py:39
  340.8 0.2 reshape.35
  341.0 25.2 %exponential_reduce_fusion = (f32[128]{0:T(128)S(1)}, f32[128]{0:T(128)S(1)}, f32[128]{0:T(128)S(1)}, f32[128,8000]{0,1:T(8,128)}) fusion(s32[128]{0:T(128)S(1)} %all-reduce, s32[8000]{0:T(1024)S(1)} %iota_add_fusion.1, f32[128,8000]{0,1:T(8,128)} %copy.12, bf16[128,3584]{1,0:T(8,128)(2,1)S(1)} %reshape.35, bf16[3584,8000]{0,1:T(8,128)(2,1)} %param.8), kind=kOutput, calls=%fused_computation.16 | convolution fusion | flops 7348224000 | bytes 66487552 | tf_op jit(solution)/shard_map/dot_general | solution.py:38
  366.2 13.9 %all-reduce.2 = (f32[128]{0:T(128)S(1)}, f32[128]{0:T(128)S(1)}, f32[128]{0:T(128)S(1)}) all-reduce(f32[128]{0:T(128)S(1)} %get-tuple-element.44, f32[128]{0:T(128)S(1)} %get-tuple-element.45, f32[128]{0:T(128)S(1)} %get-tuple-element.43), channel_id=1, replica_groups=mesh['dp'=4,'vocab'=8] {'vocab'}, use_global_device_ids=true, to_apply=%region_12.13 | all-reduce | flops 384 | bytes 3072 | tf_op jit(solution)/shard_map/psum | solution.py:14
  380.1 9.5 %all-reduce.3 = (f32[128]{0:T(128)S(1)}, f32[128]{0:T(128)S(1)}, f32[128]{0:T(128)S(1)}) all-reduce(f32[128]{0:T(128)S(1)} %get-tuple-element.56, f32[128]{0:T(128)S(1)} %get-tuple-element.57, f32[128]{0:T(128)S(1)} %get-tuple-element.58), channel_id=1, replica_groups=mesh['dp'=4,'vocab'=8] {'dp'}, use_global_device_ids=true, to_apply=%region_13.14 | all-reduce | flops 384 | bytes 3072 | tf_op jit(solution)/shard_map/psum | solution.py:14
  389.6 0.1 fusion.20
  389.7 0.6 dynamic_slice.11
  390.3 23.4 %fusion.9 = f32[128,3584]{1,0:T(8,128)S(1)} fusion(bf16[3584,8000]{0,1:T(8,128)(2,1)} %param.8, f32[128,8000]{0,1:T(8,128)} %get-tuple-element.65, f32[128,8000]{0,1:T(8,128)} %copy.12, f32[128]{0:T(128)S(1)} %get-tuple-element.64, f32[128]{0:T(128)S(1)} %get-tuple-element.62, s32[128]{0:T(128)S(1)} %all-reduce, s32[8000]{0:T(1024)S(1)} %iota_add_fusion.1), kind=kOutput, calls=%fused_computation.18 | convolution fusion | flops 7353344000 | bytes 67404544 | tf_op jit(solution)/shard_map/tv,dv->td/dot_general | solution.py:73
  413.7 57.0 %all-reduce.5 = bf16[128,3584]{1,0:T(8,128)(2,1)S(1)} all-reduce(f32[128,3584]{1,0:T(8,128)S(1)} %fusion.9), channel_id=2, replica_groups=mesh['dp'=4,'vocab'=8] {'dp','vocab'}, use_global_device_ids=true, to_apply=%region_14.15.clone | all-reduce | flops 458752 | bytes 2752512
  470.7 0.6 dynamic-slice_convert_fusion
  (20 shorter events, 0.3 us)
Async XLA Ops:
  294.5 5.6 %copy-start = (bf16[4,3584]{1,0:T(4,128)(2,1)S(1)}, bf16[4,3584]{1,0:T(4,128)(2,1)}, u32[]{:S(2)}) copy-start(bf16[4,3584]{1,0:T(4,128)(2,1)} %param.7) | copy-start | bytes 86020
